TPU v7x, 32 devices: a whole 2x2x4 slice. The times are simulated.
32 devices in a mesh: pool: 2 (over x), row: 8 (over z, y), col: 2 (over core).
Axes of the slice: x: 2, y: 2, z: 4, core: 2. Of those that a mesh axis runs over, the one named last changes fastest.
Arguments:
- grad_slots: bfloat16 [48, 256, 14336], P(('pool', 'row'), 'col'), parts along dimension 0, may hold values from -6 to 6
- block_owner: int32 [32], P('pool'), parts along dimension 0, may hold values from 0 to 7, as said below
- factor: bfloat16 [8192, 4096], P(('pool', 'col'), 'row'), parts along dimension 0, may hold values from -0.125 to 0.125
- pattern: int32 [16, 8], P('pool'), parts along dimension 0, may hold values from 0 to 1, as said below
Outputs:
- precond: bfloat16 [8192, 14336], P(('pool', 'col'), 'row'), parts along dimension 0
There are 2 independent parts, one for each index of `pool`. A program takes and returns all parts, laid end to end along the dimension named above; each array names one. Nothing has to cross between parts.
Inputs may be any that keep to these rules, and one draw needn't show every extreme that they name: `block_owner`: no trainer shard holds more than 3 blocks and one holds exactly 3; a shard keeps its blocks in its first slots in increasing block order, and the other slots are unused. `pattern`: 1 on the diagonal and 0 below it.
All inputs are finite; a program needn't handle non-finite values.
Results may differ from a plain program's by a relative error of at most 0.004.
Values may be sent and summed in bfloat16 or wider, within the bound.
A program may use at most 192 MiB of HBM per device.

v0:
```python
import jax
import jax.numpy as jnp
from jax import lax
from jax.sharding import PartitionSpec as P


def body(grad_slots, block_owner, factor, pattern):
    row_idx = lax.axis_index("row")
    col_idx = lax.axis_index("col")
    slot_cap = grad_slots.shape[0]
    block_total = block_owner.shape[0]
    received = lax.all_to_all(grad_slots, "row", split_axis=2, concat_axis=0, tiled=True)
    same_owner = block_owner[:, None] == block_owner[None, :]
    earlier = jnp.arange(block_total)[None, :] < jnp.arange(block_total)[:, None]
    owner_rank = jnp.sum(same_owner & earlier, axis=1)
    slot_of = block_owner * slot_cap + owner_rank
    picked = jnp.take(received, slot_of, axis=0)
    blocks = lax.all_gather(picked, "col", axis=1, tiled=True)
    grad_cols = blocks.reshape(-1, blocks.shape[2])
    half_rows, piece_width = factor.shape
    block_count = pattern.shape[0]
    total_rows = 2 * half_rows
    block_size = total_rows // block_count
    half_blocks = block_count // 2
    col_block = (row_idx * piece_width + jnp.arange(piece_width)) // block_size
    row_blocks = col_idx * half_blocks + jnp.arange(half_blocks)
    sel_cols = (jnp.arange(block_count)[:, None] == col_block[None, :]).astype(jnp.float32)
    pattern_cols = jnp.dot(pattern.astype(jnp.float32), sel_cols)
    sel_rows = (row_blocks[:, None] == jnp.arange(block_count)[None, :]).astype(jnp.float32)
    block_mask = jnp.dot(sel_rows, pattern_cols)
    keep_mask = block_mask > 0.5
    shaped = factor.reshape(half_blocks, block_size, piece_width)
    masked = jnp.where(keep_mask[:, None, :], shaped, jnp.zeros_like(shaped)).reshape(
        half_rows, piece_width
    )
    result = jnp.dot(
        lax.all_gather(masked, "row", axis=1, tiled=True),
        grad_cols,
        preferred_element_type=jnp.float32,
    )
    return result.astype(jnp.bfloat16)


def solution(mesh):
    placed = (
        P(("pool", "row"), "col", None),
        P("pool"),
        P(("pool", "col"), "row"),
        P("pool", None),
    )
    return jax.shard_map(
        body, mesh=mesh, in_specs=placed, out_specs=P(("pool", "col"), "row"), check_vma=False
    )
```

profile of v0, /device:TPU:0, one launch (start us, length us, event | category | flops | bytes accessed | tf_op | source)
XLA Modules:
  0.0 657.5 jit_solution(4763586861439865328)
XLA Ops:
  6.5 0.0 all-gather.3.cloned.1.call-start
  6.6 0.9 fusion.3
  7.5 3.1 bitcast_select_fusion
  10.6 0.0 all-gather.3.cloned.1.call-update
  10.6 22.4 %copy.10 = bf16[3,128,14336]{1,0,2:T(4,128)(2,1)} copy(bf16[3,128,14336]{2,1,0:T(8,128)(2,1)} %param.4) | data formatting | bytes 22020096 | tf_op args[0]
  33.0 0.0 copy-start
  33.0 7.4 %all-to-all-start = ((bf16[3,128,14336]{1,0,2:T(4,128)(2,1)}), bf16[3,128,14336]{1,0,2:T(4,128)(2,1)}, u32[]{:S(2)}, u32[]{:S(2)}) async-start(bf16[3,128,14336]{1,0,2:T(4,128)(2,1)} %copy.10), calls=%async_computation | async-start | bytes 29360128 | tf_op jit(solution)/shard_map/all_to_all | solution.py:12
  40.4 0.0 all-gather.5.cloned.1.call-start
  40.5 0.0 copy-done
  40.5 0.2 convert_reduce_fusion
  40.7 504.1 %all-to-all-done = bf16[3,128,14336]{1,0,2:T(4,128)(2,1)} async-done(((bf16[3,128,14336]{1,0,2:T(4,128)(2,1)}), bf16[3,128,14336]{1,0,2:T(4,128)(2,1)}, u32[]{:S(2)}, u32[]{:S(2)}) %all-to-all-start) | async-done | bytes 11010080 | tf_op jit(solution)/shard_map/all_to_all | solution.py:12
  544.8 12.4 %copy.11 = bf16[3,128,14336]{1,2,0:T(8,128)(2,1)} copy(bf16[3,128,14336]{1,0,2:T(4,128)(2,1)} %all-to-all-done) | data formatting | bytes 22020096 | tf_op jit(solution)/shard_map/all_to_all | solution.py:12
  557.2 14.2 %copy.12 = bf16[8,3,128,1792]{3,2,1,0:T(8,128)(2,1)} copy(bf16[8,3,128,1792]{2,3,0,1:T(8,128)(2,1)} %bitcast.9) | data formatting | bytes 22020096 | tf_op jit(solution)/shard_map/all_to_all | solution.py:12
  571.3 8.2 %gather_fusion = bf16[16,128,1792]{2,1,0:T(8,128)(2,1)} fusion(bf16[24,128,1792]{2,1,0:T(8,128)(2,1)} %bitcast.10, s32[1024]{0:T(1024)S(1)} %pad_clamp_fusion), kind=kCustom, calls=%fused_computation | custom fusion | bytes 14680128 | tf_op jit(solution)/shard_map/jit(_take)/gather | solution.py:17
  579.5 6.9 %broadcast_select_fusion = bf16[16,128,1792]{2,1,0:T(8,128)(2,1)} fusion(bf16[16,128,1792]{2,1,0:T(8,128)(2,1)} %gather_fusion, pred[16]{0:T(512)(128)(4,1)S(1)} %get-tuple-element.5), kind=kLoop, calls=%fused_computation.2 | loop fusion | flops 3670016 | bytes 14680080 | tf_op jit(solution)/shard_map/jit(_take)/select_n | solution.py:17
  586.4 0.0 all-gather.5.cloned.1.call-update
  586.5 0.0 all-gather.3.cloned.1.call-done
  586.5 25.5 %all-gather.5.cloned.1.call-done = bf16[16,256,1792]{2,1,0:T(8,128)(2,1)} async-done(((bf16[16,128,1792]{2,1,0:T(8,128)(2,1)}), bf16[16,256,1792]{2,1,0:T(8,128)(2,1)}) %all-gather.5.cloned.1.call-update) | async-done | bytes 14680080 | tf_op jit(solution)/shard_map/all_gather | solution.py:18
  612.0 38.6 %convolution_convert_fusion = bf16[2048,1792]{1,0:T(8,128)(2,1)} fusion(bf16[2048,4096]{1,0:T(8,128)(2,1)} %all-gather.3.cloned.1.call-done, bf16[4096,1792]{1,0:T(8,128)(2,1)} %bitcast.11), kind=kOutput, calls=%fused_computation.1 | convolution fusion | flops 30068441088 | bytes 38797312 | tf_op jit(solution)/shard_map/dot_general | solution.py:36
  (4 shorter events, 0.0 us)
Async XLA Ops:
  6.5 579.9 %all-gather.3.cloned.1.call-start = ((), (), s32[]{:S(2)}) async-start(), calls=%async_computation.1 | async-start | bytes 18874368 | tf_op jit(solution)/shard_map/all_gather | solution.py:37
  33.0 7.5 %copy-start = (s32[16]{0:T(128)S(1)}, s32[16]{0:T(128)}, u32[]{:S(2)}) copy-start(s32[16]{0:T(128)} %param.5) | copy-start | bytes 196
  33.0 511.8 %all-to-all-start = ((bf16[3,128,14336]{1,0,2:T(4,128)(2,1)}), bf16[3,128,14336]{1,0,2:T(4,128)(2,1)}, u32[]{:S(2)}, u32[]{:S(2)}) async-start(bf16[3,128,14336]{1,0,2:T(4,128)(2,1)} %copy.10), calls=%async_computation | async-start | bytes 29360128 | tf_op jit(solution)/shard_map/all_to_all | solution.py:12
  40.4 571.6 %all-gather.5.cloned.1.call-start = ((), (), s32[]{:S(2)}) async-start(), calls=%async_computation.2 | async-start | bytes 22020096 | tf_op jit(solution)/shard_map/all_gather | solution.py:18
Sparse Core Ops, SparseCore 0:
  10.7 526.6 all-gather.2
  586.6 25.3 all-gather.4
where the time goes:
time: 659 us; the launch traced here: 657 us
  waiting for transfers between devices  530 us (80%)
  local copies, waits for them, and re-layouts  57.2 us (9%)
  matrix products  39.5 us (6%)
  between operations  13.4 us (2%)
  other arithmetic  10.2 us (2%)
  starting transfers between devices  7.44 us (1%)
    all_to_all x1, waiting for transfers between devices, body(): lax.all_to_all(grad_slots, 'row', split_axis=2, concat_axis=0, tiled=True)  504 us
    dot_general x1, matrix products, body(): jnp.dot(lax.all_gather(masked, 'row', axis=1, tiled=True), grad_cols, pre...  38.6 us
    all_to_all x2, local copies, waits for them, and re-layouts, body(): lax.all_to_all(grad_slots, 'row', split_axis=2, concat_axis=0, tiled=True)  26.6 us
    all_gather x1, waiting for transfers between devices, body(): blocks = lax.all_gather(picked, 'col', axis=1, tiled=True)  25.5 us
    unnamed x3, local copies, waits for them, and re-layouts  22.4 us
  transfers between devices with their start and end apart: 3, of which 2 were waited for; matrix products, arithmetic and copies ran while one was open for 10% of the time, Pallas kernels for 0%

commit v1 on v0

v1 whole, which is shorter than its diff:
```python
import functools

import jax
import jax.numpy as jnp
from jax import lax
from jax.experimental import pallas as pl
from jax.experimental.pallas import tpu as pltpu
from jax.sharding import PartitionSpec as P

CHUNK = 256


def slots_of_blocks(block_owner, slot_cap):
    block_total = block_owner.shape[0]
    same_owner = block_owner[:, None] == block_owner[None, :]
    earlier = jnp.arange(block_total)[None, :] < jnp.arange(block_total)[:, None]
    owner_rank = jnp.sum(same_owner & earlier, axis=1)
    return (block_owner * slot_cap + owner_rank).astype(jnp.int32)


def masked_factor(factor, pattern):
    row_idx = lax.axis_index("row")
    col_idx = lax.axis_index("col")
    half_rows, piece_width = factor.shape
    block_count = pattern.shape[0]
    block_size = 2 * half_rows // block_count
    half_blocks = block_count // 2
    col_block = (row_idx * piece_width + jnp.arange(piece_width)) // block_size
    row_blocks = col_idx * half_blocks + jnp.arange(half_blocks)
    keep_mask = jnp.take(jnp.take(pattern, row_blocks, axis=0), col_block, axis=1) == 1
    shaped = factor.reshape(half_blocks, block_size, piece_width)
    return jnp.where(keep_mask[:, None, :], shaped, jnp.zeros_like(shaped)).reshape(
        half_rows, piece_width
    )


def plain_body(grad_slots, block_owner, factor, pattern):
    received = lax.all_to_all(grad_slots, "row", split_axis=2, concat_axis=0, tiled=True)
    slot_of = slots_of_blocks(block_owner, grad_slots.shape[0])
    picked = lax.map(lambda s: lax.dynamic_index_in_dim(received, s, 0, keepdims=False), slot_of)
    blocks = lax.all_gather(picked, "col", axis=1, tiled=True)
    grad_cols = blocks.reshape(-1, blocks.shape[2])
    result = jnp.dot(
        lax.all_gather(masked_factor(factor, pattern), "row", axis=1, tiled=True),
        grad_cols,
        preferred_element_type=jnp.float32,
    )
    return result.astype(jnp.bfloat16)


def kernel(n_row, chunks, slot_ref, grad_ref, fac_ref, out_ref, *scratch):
    recv = scratch[:chunks]
    full = scratch[chunks : 2 * chunks]
    (fbuf, stage, g_send, g_recv, own_sem, f_send, f_recv, f_own, s_send, s_recv, o_sem) = scratch[
        2 * chunks :
    ]
    me = lax.axis_index("row")
    col = lax.axis_index("col")
    slot_cap, half_tr, _ = grad_ref.shape
    width = chunks * CHUNK
    qb = fac_ref.shape[1]
    half_blocks = fac_ref.shape[0] // qb
    block_total = full[0].shape[0]
    per_block = block_total // n_row
    first = col * half_blocks

    barrier = pltpu.get_barrier_semaphore()
    for k in range(1, n_row):
        pl.semaphore_signal(
            barrier,
            inc=1,
            device_id={"row": lax.rem(me + k, n_row)},
            device_id_type=pl.DeviceIdType.MESH,
        )
    pl.semaphore_signal(
        barrier, inc=1, device_id={"col": 1 - col}, device_id_type=pl.DeviceIdType.MESH
    )
    pl.semaphore_wait(barrier, n_row)

    def flip(r, bit):
        return r + bit - 2 * bit * lax.rem(lax.div(r, bit), 2)

    bits = []
    bit = n_row // 2
    while bit >= 1:
        bits.append(bit)
        bit //= 2

    def f_copy(src, j, i, send_idx, partner):
        rows = pl.ds(i * qb, qb)
        return pltpu.make_async_remote_copy(
            src_ref=src,
            dst_ref=fbuf.at[j, rows, :],
            send_sem=f_send.at[send_idx],
            recv_sem=f_recv.at[j * half_blocks + i],
            device_id={"row": partner},
            device_id_type=pl.DeviceIdType.MESH,
        )

    def f_each(step, act):
        partner = flip(me, bits[step])
        base = (2**step - 1) * half_blocks
        for q in range(2**step):
            j = me
            for t in range(step):
                if (q >> t) & 1:
                    j = flip(j, bits[t])
            for i in range(half_blocks):
                act(j, i, base + q * half_blocks + i, partner, q)

    def f_start(step):
        def act(j, i, idx, partner, q):
            @pl.when(j >= first + i)
            def _():
                rows = pl.ds(i * qb, qb)
                src = fac_ref.at[rows, :] if q == 0 else fbuf.at[j, rows, :]
                f_copy(src, j, i, idx, partner).start()

        f_each(step, act)

    def f_wait_recv(step):
        def act(j, i, idx, partner, q):
            other = flip(j, bits[step])

            @pl.when(other >= first + i)
            def _():
                f_copy(fbuf.at[other, pl.ds(i * qb, qb), :], other, i, idx, partner).wait_recv()

        f_each(step, act)

    def f_wait_send(step):
        def act(j, i, idx, partner, q):
            @pl.when(j >= first + i)
            def _():
                f_copy(fbuf.at[j, pl.ds(i * qb, qb), :], j, i, idx, partner).wait_send()

        f_each(step, act)

    def g_copy(c, k):
        peer = lax.rem(me + k, n_row)
        cols = pl.ds(pl.multiple_of(peer * width + c * CHUNK, CHUNK), CHUNK)
        return pltpu.make_async_remote_copy(
            src_ref=grad_ref.at[:, :, cols],
            dst_ref=recv[c].at[pl.ds(me * slot_cap, slot_cap)],
            send_sem=g_send.at[c, k],
            recv_sem=g_recv.at[c, k],
            device_id={"row": peer},
            device_id_type=pl.DeviceIdType.MESH,
        )

    def own_copy(c):
        cols = pl.ds(pl.multiple_of(me * width + c * CHUNK, CHUNK), CHUNK)
        return pltpu.make_async_copy(
            grad_ref.at[:, :, cols],
            recv[c].at[pl.ds(me * slot_cap, slot_cap)],
            own_sem.at[c],
        )

    order = sorted(range(1, n_row), key=lambda k: abs(k - n_row // 2))

    def g_start(c):
        for k in order:
            g_copy(c, k).start()
        own_copy(c).start()

    def g_wait(c):
        for k in order:
            src = lax.rem(me + n_row - k, n_row)
            pltpu.make_async_remote_copy(
                src_ref=recv[c].at[pl.ds(src * slot_cap, slot_cap)],
                dst_ref=recv[c].at[pl.ds(src * slot_cap, slot_cap)],
                send_sem=g_send.at[c, k],
                recv_sem=g_recv.at[c, k],
                device_id={"row": src},
                device_id_type=pl.DeviceIdType.MESH,
            ).wait_recv()
        own_copy(c).wait()

    half = pl.ds(pl.multiple_of(col * half_tr, half_tr), half_tr)

    def s_copy(c):
        return pltpu.make_async_remote_copy(
            src_ref=full[c].at[:, half, :],
            dst_ref=full[c].at[:, half, :],
            send_sem=s_send.at[c],
            recv_sem=s_recv.at[c],
            device_id={"col": 1 - col},
            device_id_type=pl.DeviceIdType.MESH,
        )

    def pick(c):
        def body(b, carry):
            full[c][b, half, :] = recv[c][slot_ref[b]]
            return carry

        lax.fori_loop(0, block_total, body, 0)

    def o_copy(c):
        return pltpu.make_async_copy(
            stage.at[c % 2], out_ref.at[:, pl.ds(c * CHUNK, CHUNK)], o_sem.at[c % 2]
        )

    def compute(c):
        s_copy(c).wait_recv()
        if c >= 2:
            o_copy(c - 2).wait()

        def rows_body(i, carry):
            rows = pl.ds(pl.multiple_of(i * qb, qb), qb)

            def dot_body(j, acc):
                g = full[c][pl.ds(j * per_block, per_block)].reshape(qb, CHUNK)
                return acc + jnp.dot(fbuf[j, rows, :], g, preferred_element_type=jnp.float32)

            acc = lax.fori_loop(first + i, n_row, dot_body, jnp.zeros((qb, CHUNK), jnp.float32))
            stage[c % 2, rows, :] = acc.astype(jnp.bfloat16)
            return carry

        lax.fori_loop(0, half_blocks, rows_body, 0)
        o_copy(c).start()

    fown_copy = pltpu.make_async_copy(fac_ref, fbuf.at[me], f_own)
    f_start(0)
    g_start(0)
    fown_copy.start()
    started = 1
    for step in range(len(bits)):
        if started < chunks:
            g_start(started)
            started += 1
        f_wait_recv(step)
        if step + 1 < len(bits):
            f_start(step + 1)
    fown_copy.wait()
    while started < chunks:
        g_start(started)
        started += 1
    for c in range(chunks):
        g_wait(c)
        pick(c)
        s_copy(c).start()
        if c >= 1:
            compute(c - 1)
    compute(chunks - 1)
    for c in range(chunks):
        for k in order:
            g_copy(c, k).wait_send()
        s_copy(c).wait_send()
    for step in range(len(bits)):
        f_wait_send(step)
    for c in range(max(chunks - 2, 0), chunks):
        o_copy(c).wait()


def kernel_body(n_row, grad_slots, block_owner, factor, pattern):
    slot_cap, half_tr, total_width = grad_slots.shape
    chunks = total_width // n_row // CHUNK
    half_rows, qb = factor.shape
    half_blocks = half_rows // qb
    block_total = block_owner.shape[0]
    slot_of = slots_of_blocks(block_owner, slot_cap)
    masked = masked_factor(factor, pattern)
    dma = pltpu.SemaphoreType.DMA
    return pl.pallas_call(
        functools.partial(kernel, n_row, chunks),
        out_shape=jax.ShapeDtypeStruct((half_rows, chunks * CHUNK), jnp.bfloat16),
        in_specs=[
            pl.BlockSpec(memory_space=pltpu.SMEM),
            pl.BlockSpec(memory_space=pl.ANY),
            pl.BlockSpec(memory_space=pl.ANY),
        ],
        out_specs=pl.BlockSpec(memory_space=pl.ANY),
        scratch_shapes=[pltpu.VMEM((n_row * slot_cap, half_tr, CHUNK), jnp.bfloat16)] * chunks
        + [pltpu.VMEM((block_total, 2 * half_tr, CHUNK), jnp.bfloat16)] * chunks
        + [
            pltpu.VMEM((n_row, half_rows, qb), jnp.bfloat16),
            pltpu.VMEM((2, half_rows, CHUNK), jnp.bfloat16),
            dma((chunks, n_row)),
            dma((chunks, n_row)),
            dma((chunks,)),
            dma(((n_row - 1) * half_blocks,)),
            dma((n_row * half_blocks,)),
            dma,
            dma((chunks,)),
            dma((chunks,)),
            dma((2,)),
        ],
        compiler_params=pltpu.CompilerParams(
            collective_id=0, has_side_effects=True, vmem_limit_bytes=58 * 2**20
        ),
        cost_estimate=pl.CostEstimate(
            flops=2 * half_rows * n_row * qb * chunks * CHUNK,
            bytes_accessed=4 * half_rows * chunks * CHUNK,
            transcendentals=0,
        ),
    )(slot_of, grad_slots, masked)


def solution(mesh):
    placed = (
        P(("pool", "row"), "col", None),
        P("pool"),
        P(("pool", "col"), "row"),
        P("pool", None),
    )
    n_row = mesh.shape["row"]

    def body(grad_slots, block_owner, factor, pattern):
        width = grad_slots.shape[2] // n_row
        half_tr = grad_slots.shape[1]
        one_block = factor.shape[1] * pattern.shape[0] == 2 * factor.shape[0]
        power = n_row & (n_row - 1) == 0
        whole = (block_owner.shape[0] * 2 * half_tr) % (n_row * 2 * half_tr) == 0
        tiled = width % CHUNK == 0 and half_tr % 16 == 0 and pattern.shape[0] == n_row
        if one_block and power and whole and tiled:
            return kernel_body(n_row, grad_slots, block_owner, factor, pattern)
        return plain_body(grad_slots, block_owner, factor, pattern)

    return jax.shard_map(
        body, mesh=mesh, in_specs=placed, out_specs=P(("pool", "col"), "row"), check_vma=False
    )
```

time: 659 us -> 450 us (0.68)
  waiting for transfers between devices: 530 us -> 0 us
  Pallas kernels: 0 us -> 436 us
  local copies, waits for them, and re-layouts: 57.2 us -> 8.4 us
  matrix products: 39.5 us -> 0 us
  between operations: 13.4 us -> 0.07 us
  starting transfers between devices: 7.44 us -> 0 us
    all_to_all x1 -> x0, waiting for transfers between devices: 504 us -> none  [body(): lax.all_to_all(grad_slots, 'row', split_axis=2, concat_axis=0, tiled=True)]
    pallas_call x0 -> x1, Pallas kernels: none -> 436 us  [kernel_body(): pl.pallas_call(functools.partial(kernel, n_row, chunks), out_shape=jax.Sh...]
    dot_general x2 -> x0, matrix products: 39.5 us -> none  [the longest x1 38.6 us: body(): jnp.dot(lax.all_gather(masked, 'row', axis=1, tiled=True), grad_cols, pre...]
    all_to_all x2 -> x0, local copies, waits for them, and re-layouts: 26.6 us -> none  [body(): lax.all_to_all(grad_slots, 'row', split_axis=2, concat_axis=0, tiled=True)]
    all_gather x2 -> x0, waiting for transfers between devices: 25.5 us -> none  [the longest x1 25.5 us: body(): blocks = lax.all_gather(picked, 'col', axis=1, tiled=True)]
    unnamed x3, local copies, waits for them, and re-layouts: 22.4 us -> 6.61 us
    all_to_all x1 -> x0, starting transfers between devices: 7.4 us -> none  [body(): lax.all_to_all(grad_slots, 'row', split_axis=2, concat_axis=0, tiled=True)]
    select_n x3 -> x4, other arithmetic: 10 us -> 3.17 us  [the longest x1 3.07 us: masked_factor(): jnp.where(keep_mask[:, None, :], shaped, jnp.zeros_like(shaped))]
  transfers between devices with their start and end apart: 3 -> 0, of which waited for: 2 -> 0; matrix products, arithmetic and copies ran while one was open for 10% -> 0% of each run, Pallas kernels for 0% -> 0%
where the time goes in v1:
time: 450 us
  Pallas kernels  436 us (97%)
  local copies, waits for them, and re-layouts  8.4 us (2%)
  other arithmetic  5.51 us (1%)
    pallas_call x1, Pallas kernels, kernel_body(): pl.pallas_call(functools.partial(kernel, n_row, chunks), out_shape=jax.Sh...  436 us

profile of v1, /device:TPU:0, one launch (start us, length us, event | category | flops | bytes accessed | tf_op | source)
XLA Modules:
  0.0 449.7 jit_solution(6609451201767695697)
XLA Ops:
  0.0 0.0 copy-start
  0.0 0.9 convert_reduce_fusion
  0.9 1.3 multiply_add_fusion.slot_ref
  2.3 0.0 copy-done
  2.3 0.6 gather_fusion
  2.8 0.1 broadcast_select_fusion
  2.9 0.1 copy.9
  3.0 1.0 gather_fusion.1
  4.0 0.1 fusion
  4.2 0.1 copy.10
  4.3 3.1 bitcast_select_fusion.fac_ref
  7.4 435.7 %shard_map.46 = bf16[2048,1792]{1,0:T(8,128)(2,1)} custom-call(s32[16]{0:T(128)} %multiply_add_fusion.slot_ref, bf16[3,128,14336]{2,1,0:T(8,128)(2,1)} %grad_ref.1, bf16[2048,512]{1,0:T(8,128)(2,1)} %bitcast_select_fusion.fac_ref), custom_call_target="tpu_custom_call" | custom-call | flops 30064771072 | bytes 14680064 | tf_op jit(solution)/shard_map/pallas_call | solution.py:264
  443.1 6.6 %copy.12 = bf16[2048,1792]{1,0:T(8,128)(2,1)} copy(bf16[2048,1792]{1,0:T(8,128)(2,1)} %shard_map.46) | data formatting | bytes 14680064
  (6 shorter events, 0.1 us)
Async XLA Ops:
  0.0 2.3 copy-start

commit v2 on v1

--- a/solution.py
+++ b/solution.py
@@ -156,11 +156,13 @@
             own_sem.at[c],
         )
 
-    order = sorted(range(1, n_row), key=lambda k: abs(k - n_row // 2))
+    by_reach = sorted(range(1, n_row), key=lambda k: abs(k - n_row // 2))
+    order = [by_reach[t // 2 if t % 2 == 0 else n_row - 2 - t // 2] for t in range(n_row - 1)]
 
     def g_start(c):
-        for k in order:
-            g_copy(c, k).start()
+        for t in range(n_row - 1):
+            near, far = order[t], order[(t + 1) % (n_row - 1)]
+            g_copy(c, near + col * (far - near)).start()
         own_copy(c).start()
 
     def g_wait(c):
@@ -220,20 +222,29 @@
         o_copy(c).start()
 
     fown_copy = pltpu.make_async_copy(fac_ref, fbuf.at[me], f_own)
+    def g_start_on(which, c):
+        @pl.when(col == which)
+        def _():
+            g_start(c)
+
     f_start(0)
-    g_start(0)
+    g_start_on(0, 0)
+    for c in range(min(4, chunks)):
+        g_start_on(1, c)
     fown_copy.start()
     started = 1
     for step in range(len(bits)):
         if started < chunks:
-            g_start(started)
+            g_start_on(0, started)
             started += 1
         f_wait_recv(step)
         if step + 1 < len(bits):
             f_start(step + 1)
     fown_copy.wait()
+    for c in range(min(4, chunks), chunks):
+        g_start_on(1, c)
     while started < chunks:
-        g_start(started)
+        g_start_on(0, started)
         started += 1
     for c in range(chunks):
         g_wait(c)

time: 450 us -> 434 us (0.964)
  Pallas kernels: 436 us -> 420 us
    pallas_call x1, Pallas kernels: 436 us -> 420 us  [kernel_body(): pl.pallas_call(functools.partial(kernel, n_row, chunks), out_shape=jax.Sh...]
where the time goes in v2:
time: 434 us
  Pallas kernels  420 us (97%)
  local copies, waits for them, and re-layouts  8.4 us (2%)
  other arithmetic  5.51 us (1%)
    pallas_call x1, Pallas kernels, kernel_body(): pl.pallas_call(functools.partial(kernel, n_row, chunks), out_shape=jax.Sh...  420 us

profile of v2, /device:TPU:0, one launch (start us, length us, event | category | flops | bytes accessed | tf_op | source)
XLA Modules:
  0.0 433.8 jit_solution(2881059182807757733)
XLA Ops:
  0.0 0.0 copy-start
  0.0 0.9 convert_reduce_fusion
  0.9 1.3 multiply_add_fusion.slot_ref
  2.3 0.0 copy-done
  2.3 0.6 gather_fusion
  2.8 0.1 broadcast_select_fusion
  2.9 0.1 copy.9
  3.0 1.0 gather_fusion.1
  4.0 0.1 fusion
  4.2 0.1 copy.10
  4.3 3.1 bitcast_select_fusion.fac_ref
  7.4 419.8 %shard_map.46 = bf16[2048,1792]{1,0:T(8,128)(2,1)} custom-call(s32[16]{0:T(128)} %multiply_add_fusion.slot_ref, bf16[3,128,14336]{2,1,0:T(8,128)(2,1)} %grad_ref.1, bf16[2048,512]{1,0:T(8,128)(2,1)} %bitcast_select_fusion.fac_ref), custom_call_target="tpu_custom_call" | custom-call | flops 30064771072 | bytes 14680064 | tf_op jit(solution)/shard_map/pallas_call | solution.py:275
  427.2 6.6 %copy.12 = bf16[2048,1792]{1,0:T(8,128)(2,1)} copy(bf16[2048,1792]{1,0:T(8,128)(2,1)} %shard_map.46) | data formatting | bytes 14680064
  (6 shorter events, 0.1 us)
Async XLA Ops:
  0.0 2.3 copy-start
